TPU v7x, 512 devices: a whole 4x4x16 slice. The times are simulated.
512 devices in a mesh: seq: 32 (over z, core), head: 4 (over x), dp: 4 (over y).
Axes of the slice: x: 4, y: 4, z: 16, core: 2. Of those that a mesh axis runs over, the one named last changes fastest.
Arguments:
- passthrough: bfloat16 [4, 8192, 1024], P('dp', 'seq', 'head'), may hold values from -6 to 6
- mixed_out: bfloat16 [4, 8192, 1024], P('dp', 'seq', 'head'), may hold values from -6 to 6
- grad_mixed: bfloat16 [4, 8192, 1024], P('dp', 'seq', 'head'), may hold values from -6 to 6
- grad_pass: bfloat16 [4, 8192, 1024], P('dp', 'seq', 'head'), may hold values from -6 to 6
- query_weight: bfloat16 [1024, 1024], P(None, 'head'), may hold values from -0.1875 to 0.1875
- key_weight: bfloat16 [1024, 1024], P(None, 'head'), may hold values from -0.1875 to 0.1875
- value_weight: bfloat16 [1024, 1024], P(None, 'head'), may hold values from -0.1875 to 0.1875
- random_features: bfloat16 [8, 128, 256], P('head'), may hold values from -5 to 5
- document_ids: int32 [4, 8192], P('dp', 'seq'), may hold values from 0 to 27, never falling along the last dimension, each value on 1 to 2048 neighbouring positions
Outputs:
- first_in: bfloat16 [4, 8192, 1024], P('dp', 'seq', 'head')
- grad_second: bfloat16 [4, 8192, 1024], P('dp', 'seq', 'head')
- grad_query_weight: float32 [1024, 1024], P(('seq', 'dp'), 'head')
- grad_key_weight: float32 [1024, 1024], P(('seq', 'dp'), 'head')
- grad_value_weight: float32 [1024, 1024], P(('seq', 'dp'), 'head')
Inputs may be any that keep to these rules, and one draw needn't show every extreme that they name: `document_ids`: along each context the number never falls; each of the 28 documents holds 1 to 2048 positions, and one holds exactly 2048.
All inputs are finite; a program needn't handle non-finite values.
Results may differ from a plain program's by a relative error of at most 0.018.
The roundings to bfloat16 on the way count: a program that leaves them out, or rounds other values in their place, can miss the bound.
Values may be sent and summed in bfloat16 or wider, within the bound.
A program may use at most 64 MiB of HBM per device.

v0:
```python
import jax
import jax.numpy as jnp
from jax import lax
from jax.sharding import PartitionSpec as P

EPSILON = 1e-06
HIGHEST = lax.Precision.HIGHEST


def carried_in(array, axis, join, neutral, backward):
    count = lax.axis_size(axis)
    place = lax.axis_index(axis)
    ahead = count - 1 - place if backward else place
    gathered = jax.tree.map(
        lambda a, kind: lax.all_gather(a.astype(kind), axis), array, (jnp.bfloat16, jnp.bfloat16)
    )
    state = jax.tree.map(lambda a, e: jnp.zeros_like(a) + jnp.asarray(e, a.dtype), array, neutral)

    def one(turn, state):
        source = count - 1 - turn if backward else turn
        return join(
            state,
            jax.tree.map(
                lambda a, own: lax.dynamic_index_in_dim(a, source, 0, False).astype(own.dtype),
                gathered,
                array,
            ),
        )

    return lax.fori_loop(0, ahead, one, state)


def to_heads(matrix, head_count):
    count_ctx, tok_rows, columns = matrix.shape
    return matrix.reshape(count_ctx, tok_rows, head_count, columns // head_count).transpose(
        0, 2, 1, 3
    )


def from_heads(tensor):
    count_ctx, head_count, tok_rows, head_dim = tensor.shape
    return tensor.transpose(0, 2, 1, 3).reshape(count_ctx, tok_rows, head_count * head_dim)


def feature_map(projected, random_features):
    head_dim = projected.shape[-1]
    mixing = jnp.einsum(
        "chtd,hdm->chtm", projected, random_features, preferred_element_type=jnp.float32
    )
    widened = projected.astype(jnp.float32)
    squares = jnp.sum(widened * widened, axis=-1, keepdims=True)
    exponent = mixing / head_dim**0.25 - squares / (2.0 * head_dim**0.5)
    return (jnp.exp(exponent) / random_features.shape[-1] ** 0.5).astype(jnp.bfloat16)


def feature_grad(dfeature, feature, projected, random_features):
    head_dim = projected.shape[-1]
    dexponent = dfeature * feature.astype(jnp.float32)
    rounded = dexponent.astype(jnp.bfloat16)
    back_proj = jnp.einsum(
        "chtm,hdm->chtd", rounded, random_features, preferred_element_type=jnp.float32
    )
    totals = jnp.sum(dexponent, axis=-1, keepdims=True)
    result = back_proj / head_dim**0.25 - projected.astype(jnp.float32) * totals / head_dim**0.5
    return result.astype(jnp.bfloat16)


def join_state(earlier, later_part):
    early_state, early_id = earlier
    late_state, late_id = later_part
    same_id = (early_id == late_id)[:, None, None, None]
    vacant = (late_id < 0.0)[:, None, None, None]
    merged = jnp.where(vacant, early_state, late_state + jnp.where(same_id, early_state, 0.0))
    new_id = jnp.where(late_id < 0.0, early_id, late_id)
    return (merged, new_id)


def shards(
    passthrough,
    mixed_out,
    grad_mixed,
    grad_pass,
    query_weight,
    key_weight,
    value_weight,
    random_features,
    document_ids,
):
    head_count = random_features.shape[0]
    count_ctx, tok_rows, local_width = passthrough.shape
    whole_in = lax.all_gather(passthrough, "head", axis=2, tiled=True)
    widened = whole_in.astype(jnp.float32)
    full_width = widened.shape[2]
    inv_rms = lax.rsqrt(jnp.mean(widened * widened, axis=2, keepdims=True) + EPSILON)
    normed = (widened * inv_rms).astype(jnp.bfloat16)
    query_proj = jnp.einsum(
        "ctd,dj->ctj", normed, query_weight, preferred_element_type=jnp.float32
    ).astype(jnp.bfloat16)
    key_proj = jnp.einsum(
        "ctd,dj->ctj", normed, key_weight, preferred_element_type=jnp.float32
    ).astype(jnp.bfloat16)
    value_proj = jnp.einsum(
        "ctd,dj->ctj", normed, value_weight, preferred_element_type=jnp.float32
    ).astype(jnp.bfloat16)
    query_heads = to_heads(query_proj, head_count)
    key_heads = to_heads(key_proj, head_count)
    value_heads = to_heads(value_proj, head_count)
    feat_query = feature_map(query_heads, random_features)
    feat_key = feature_map(key_heads, random_features)
    ids_wide = document_ids.astype(jnp.float32)
    rows_idx = lax.broadcasted_iota(jnp.int32, (tok_rows, tok_rows), 0)
    cols_idx = lax.broadcasted_iota(jnp.int32, (tok_rows, tok_rows), 1)
    same_doc = document_ids[:, :, None] == document_ids[:, None, :]
    allowed = (same_doc & (rows_idx >= cols_idx)[None])[:, None]
    scores = jnp.einsum("chtm,chsm->chts", feat_query, feat_key, preferred_element_type=jnp.float32)
    pair_weight = jnp.where(allowed, scores, 0.0).astype(jnp.bfloat16)
    attn_local = jnp.einsum(
        "chts,chsd->chtd", pair_weight, value_heads, preferred_element_type=jnp.float32
    )
    last_ids = ids_wide[:, -1]
    tail_mask = (ids_wide == last_ids[:, None])[:, None, :, None]
    tail_keys = jnp.where(tail_mask, feat_key, jnp.zeros_like(feat_key))
    tail_state = jnp.einsum(
        "chtm,chtd->chmd", tail_keys, value_heads, preferred_element_type=jnp.float32
    )
    empty_state = (jnp.zeros_like(tail_state), jnp.full_like(last_ids, -1.0))
    state_in, state_id = carried_in((tail_state, last_ids), "seq", join_state, empty_state, False)
    head_on = (ids_wide == state_id[:, None])[:, None, :, None]
    fq_wide = feat_query.astype(jnp.float32)
    carried = jnp.einsum("chtm,chmd->chtd", fq_wide, state_in, precision=HIGHEST)
    attention = attn_local + jnp.where(head_on, carried, 0.0)
    inv_attn = lax.rsqrt(jnp.mean(attention * attention, axis=-1, keepdims=True) + EPSILON)
    act = attention * inv_attn
    first_in = (mixed_out.astype(jnp.float32) - from_heads(act)).astype(jnp.bfloat16)
    grad_act = to_heads(grad_mixed, head_count).astype(jnp.float32)
    grad_attn = (
        inv_attn * (grad_act - act * jnp.mean(grad_act * act, axis=-1, keepdims=True))
    ).astype(jnp.bfloat16)
    dscores = jnp.einsum(
        "chtd,chsd->chts", grad_attn, value_heads, preferred_element_type=jnp.float32
    )
    dpair = jnp.where(allowed, dscores, 0.0).astype(jnp.bfloat16)
    first_ids = ids_wide[:, 0]
    head_mask = (ids_wide == first_ids[:, None])[:, None, :, None]
    head_query = jnp.where(head_mask, feat_query, jnp.zeros_like(feat_query))
    head_state = jnp.einsum(
        "chtm,chtd->chmd", head_query, grad_attn, preferred_element_type=jnp.float32
    )
    state_later, later_id = carried_in(
        (head_state, first_ids), "seq", join_state, empty_state, True
    )
    tail_on = (ids_wide == later_id[:, None])[:, None, :, None]
    grad_wide = grad_attn.astype(jnp.float32)
    dfeat_query = jnp.einsum("chts,chsm->chtm", dpair, feat_key, preferred_element_type=jnp.float32)
    dfeat_query = dfeat_query + jnp.where(
        head_on, jnp.einsum("chtd,chmd->chtm", grad_wide, state_in, precision=HIGHEST), 0.0
    )
    dfeat_key = jnp.einsum("chts,chtm->chsm", dpair, feat_query, preferred_element_type=jnp.float32)
    dfeat_key = dfeat_key + jnp.where(
        tail_on,
        jnp.einsum(
            "chsd,chmd->chsm", value_heads.astype(jnp.float32), state_later, precision=HIGHEST
        ),
        0.0,
    )
    dvalue = jnp.einsum(
        "chts,chtd->chsd", pair_weight, grad_attn, preferred_element_type=jnp.float32
    )
    dvalue = dvalue + jnp.where(
        tail_on,
        jnp.einsum("chsm,chmd->chsd", feat_key.astype(jnp.float32), state_later, precision=HIGHEST),
        0.0,
    )
    dvalue = dvalue.astype(jnp.bfloat16)
    dquery = feature_grad(dfeat_query, feat_query, query_heads, random_features)
    dkey = feature_grad(dfeat_key, feat_key, key_heads, random_features)
    grads_flat = jnp.concatenate([from_heads(dquery), from_heads(dkey), from_heads(dvalue)], axis=2)
    weights_all = jnp.concatenate([query_weight, key_weight, value_weight], axis=1)
    partial_value = jnp.einsum(
        "ctj,dj->ctd", grads_flat, weights_all, preferred_element_type=jnp.float32
    )
    grad_normed = lax.psum_scatter(
        partial_value.astype(jnp.bfloat16), "head", scatter_dimension=2, tiled=True
    ).astype(jnp.float32)
    norm_local = passthrough.astype(jnp.float32) * inv_rms
    dot_sum = lax.psum(jnp.sum(grad_normed * norm_local, axis=2), "head")
    grad_second = grad_pass.astype(jnp.float32) + inv_rms * (
        grad_normed - norm_local * (dot_sum / full_width)[:, :, None]
    )
    grad_second = grad_second.astype(jnp.bfloat16)
    seq_count = lax.axis_size("seq")
    dp_count = lax.axis_size("dp")
    total_rows = count_ctx * tok_rows * seq_count * dp_count
    grad_scale = 1.0 / total_rows**0.5
    summed = lax.psum_scatter(
        jnp.einsum("ctr,ctj->rj", normed, grads_flat, preferred_element_type=jnp.float32)
        * grad_scale,
        ("seq", "dp"),
        scatter_dimension=0,
        tiled=True,
    )
    return (
        first_in,
        grad_second,
        summed[:, :local_width],
        summed[:, local_width : 2 * local_width],
        summed[:, 2 * local_width :],
    )


def solution(mesh):
    placed = (
        P("dp", "seq", "head"),
        P("dp", "seq", "head"),
        P("dp", "seq", "head"),
        P("dp", "seq", "head"),
        P(None, "head"),
        P(None, "head"),
        P(None, "head"),
        P("head", None, None),
        P("dp", "seq"),
    )
    return jax.shard_map(
        shards,
        mesh=mesh,
        in_specs=placed,
        out_specs=(
            P("dp", "seq", "head"),
            P("dp", "seq", "head"),
            P(("seq", "dp"), "head"),
            P(("seq", "dp"), "head"),
            P(("seq", "dp"), "head"),
        ),
        check_vma=False,
    )
```

profile of v0, /device:TPU:2, one launch (start us, length us, event | category | flops | bytes accessed | tf_op | source)
XLA Modules:
  0.0 698.9 jit_solution(1416142091037650247)
XLA Ops:
  8.6 15.7 %all_gather.23 = bf16[1,256,1024]{2,1,0:T(8,128)(2,1)S(1)} all-gather(bf16[1,256,256]{2,1,0:T(8,128)(2,1)} %param.13), channel_id=1, replica_groups=mesh['seq'=32,'head'=4,'dp'=4] {'head'}, dimensions={2}, use_global_device_ids=true | all-gather | bytes 655360 | tf_op jit(solution)/shard_map/all_gather | solution.py:91
  24.6 1.5 convolution_convert_fusion.3
  26.1 1.5 convolution_convert_fusion.2
  27.7 1.3 compare_reduce_fusion.1
  31.7 1.3 dynamic-slice
  34.4 50.4 %all-reduce.2 = (bf16[32]{0:T(256)(128)(2,1)S(1)}, bf16[32]{0:T(256)(128)(2,1)S(1)}) all-reduce(bf16[32]{0:T(256)(128)(2,1)S(1)} %dynamic-update-slice, bf16[32]{0:T(256)(128)(2,1)S(1)} %dynamic-update-slice.1), channel_id=1, replica_groups=mesh['seq'=32,'head'=4,'dp'=4] {'seq'}, use_global_device_ids=true, to_apply=%add | all-reduce | flops 64 | bytes 256
  86.1 20.5 %all-gather.5.cloned.1.call-done = bf16[64,256,128]{2,1,0:T(8,128)(2,1)} async-done(((bf16[2,256,128]{2,1,0:T(8,128)(2,1)}), bf16[64,256,128]{2,1,0:T(8,128)(2,1)}) %all-gather.5.cloned.1.call-update) | async-done | bytes 4194320 | tf_op jit(solution)/shard_map/all_gather | solution.py:15
  110.0 177.3 %all-gather.7.cloned.1.call-done = bf16[64,256,128]{2,1,0:T(8,128)(2,1)} async-done(((bf16[2,256,128]{2,1,0:T(8,128)(2,1)}), bf16[64,256,128]{2,1,0:T(8,128)(2,1)}) %all-gather.7.cloned.1.call-update) | async-done | bytes 4194320 | tf_op jit(solution)/shard_map/all_gather | solution.py:15
  287.3 111.8 %while.27 = (s32[]{:T(128)}, f32[1,2,256,128]{3,2,1,0:T(8,128)S(1)}, f32[1]{0:T(128)}, s32[]{:T(128)}, bf16[32,1]{0,1:T(2,128)(2,1)S(1)}, /*index=5*/bf16[32,1,2...) while((s32[]{:T(128)}, ...), condition=%wide.region_9.10_spmd, body=%wide.region_8.9_spmd.sunk | while | flops 262153 | bytes 655570 | solution.py:30
  289.8 1.0 fusion.111
  293.4 1.0 fusion.111
  297.0 1.0 fusion.111
  300.6 1.0 fusion.111
  304.3 1.0 fusion.111
  307.9 1.0 fusion.111
  311.5 1.0 fusion.111
  400.2 2.8 fusion.11
  403.1 2.4 convolution_multiply_fusion
  406.4 15.4 %reduce-scatter.3.cloned.1.call-done = bf16[1,256,256]{2,1,0:T(8,128)(2,1)} async-done(((bf16[1,256,1024]{2,1,0:T(8,128)(2,1)}), bf16[1,256,256]{2,1,0:T(8,128)(2,1)}) %reduce-scatter.3.cloned.1.call-update) | async-done | bytes 131088 | tf_op jit(solution)/shard_map/reduce_scatter | solution.py:182
  421.8 1.1 fusion.43
  422.9 9.7 %psum.7 = f32[1,256]{1,0:T(1,128)S(1)} all-reduce(f32[1,256]{1,0:T(1,128)S(1)} %bitcast.261), channel_id=1, replica_groups=mesh['seq'=32,'head'=4,'dp'=4] {'head'}, use_global_device_ids=true, to_apply=%region_13.14 | all-reduce | flops 256 | bytes 2048 | tf_op jit(solution)/shard_map/psum | solution.py:186
  432.6 1.7 fusion.46
  434.3 256.8 %reduce-scatter.5.cloned.1.call-done = f32[8,768]{1,0:T(8,128)} async-done(((f32[1024,768]{1,0:T(8,128)}), f32[8,768]{1,0:T(8,128)}) %reduce-scatter.5.cloned.1.call-update) | async-done | bytes 24592 | tf_op jit(solution)/shard_map/reduce_scatter | solution.py:195
  691.1 1.3 fusion.85
  (121 shorter events, 54.3 us)
Async XLA Ops:
  7.2 21.8 %copy-start = (bf16[2,128,256]{2,1,0:T(8,128)(2,1)S(1)}, bf16[2,128,256]{2,1,0:T(8,128)(2,1)}, u32[]{:S(2)}) copy-start(bf16[2,128,256]{2,1,0:T(8,128)(2,1)} %param.20) | copy-start | bytes 393220
  7.2 20.5 %copy-start.5 = (s32[1,256]{1,0:T(1,128)S(1)}, s32[1,256]{1,0:T(1,128)}, u32[]{:S(2)}) copy-start(s32[1,256]{1,0:T(1,128)} %param.21) | copy-start | bytes 3076
  7.2 24.4 %copy-start.2 = (bf16[1,256,256]{2,1,0:T(8,128)(2,1)S(1)}, bf16[1,256,256]{2,1,0:T(8,128)(2,1)}, u32[]{:S(2)}) copy-start(bf16[1,256,256]{2,1,0:T(8,128)(2,1)} %param.15) | copy-start | bytes 393220
  7.2 77.7 %copy-start.6 = (bf16[1024,256]{1,0:T(8,128)(2,1)S(1)}, bf16[1024,256]{1,0:T(8,128)(2,1)}, u32[]{:S(2)}) copy-start(bf16[1024,256]{1,0:T(8,128)(2,1)} %param.17) | copy-start | bytes 1572868
  7.2 99.4 %all-gather.5.cloned.1.call-start = ((), (), s32[]{:S(2)}) async-start(), calls=%async_computation.4 | async-start | bytes 4325376 | tf_op jit(solution)/shard_map/all_gather | solution.py:15
  30.2 257.0 %all-gather.7.cloned.1.call-start = ((), (), s32[]{:S(2)}) async-start(), calls=%async_computation.5 | async-start | bytes 4325376 | tf_op jit(solution)/shard_map/all_gather | solution.py:15
  108.3 313.4 %reduce-scatter.3.cloned.1.call-start = ((), (), s32[]{:S(2)}) async-start(), calls=%async_computation.2 | async-start | bytes 655360 | tf_op jit(solution)/shard_map/reduce_scatter | solution.py:182
  403.0 2.6 copy-start.3
  403.1 18.7 %copy-start.1 = (bf16[1,256,256]{2,1,0:T(8,128)(2,1)S(1)}, bf16[1,256,256]{2,1,0:T(8,128)(2,1)}, u32[]{:S(2)}) copy-start(bf16[1,256,256]{2,1,0:T(8,128)(2,1)} %param.13) | copy-start | bytes 393220
  403.1 288.0 %reduce-scatter.5.cloned.1.call-start = ((), (), s32[]{:S(2)}) async-start(), calls=%async_computation.3 | async-start | bytes 3170304 | tf_op jit(solution)/shard_map/reduce_scatter | solution.py:195
  405.5 27.1 %copy-start.4 = (bf16[1,256,256]{2,1,0:T(8,128)(2,1)S(1)}, bf16[1,256,256]{2,1,0:T(8,128)(2,1)}, u32[]{:S(2)}) copy-start(bf16[1,256,256]{2,1,0:T(8,128)(2,1)} %param.16) | copy-start | bytes 393220
Sparse Core Ops, SparseCore 0:
  30.3 76.2 all-gather.4
  109.3 177.9 all-gather.6
  403.2 18.5 reduce-scatter.2
  426.3 264.7 reduce-scatter.4
where the time goes:
time: 701 us; the launch traced here: 699 us
  waiting for transfers between devices  470 us (67%)
  blocking collectives  75.9 us (11%)
  loops' own time  61.4 us (9%)
  other arithmetic  38.4 us (5%)
  local copies, waits for them, and re-layouts  23.3 us (3%)
  between operations  15.4 us (2%)
  matrix products  14.5 us (2%)
    reduce_scatter x1, waiting for transfers between devices, shards(): lax.psum_scatter(jnp.einsum('ctr,ctj->rj', normed, grads_flat, preferred_...  257 us
    all_gather x2, waiting for transfers between devices, carried_in(): lax.all_gather(a.astype(kind), axis)  198 us
    another operation x2, loops' own time, carried_in(): return lax.fori_loop(0, ahead, one, state)  61.4 us
    unnamed x1, blocking collectives  50.4 us
    select_n x31, other arithmetic, join_state(): jnp.where(vacant, early_state, late_state + jnp.where(same_id, early_stat...  32.2 us
    dynamic_slice x31, local copies, waits for them, and re-layouts, one(): lax.dynamic_index_in_dim(a, source, 0, False).astype(own.dtype)  18.2 us
    all_gather x1, blocking collectives, shards(): whole_in = lax.all_gather(passthrough, 'head', axis=2, tiled=True)  15.7 us
    reduce_scatter x1, waiting for transfers between devices, shards(): lax.psum_scatter(partial_value.astype(jnp.bfloat16), 'head', scatter_dime...  15.4 us
  transfers between devices with their start and end apart: 4, of which 4 were waited for; matrix products, arithmetic and copies ran while one was open for 2% of the time, Pallas kernels for 0%

commit v1 on v0

--- a/solution.py
+++ b/solution.py
@@ -88,7 +88,10 @@
 ):
     head_count = random_features.shape[0]
     count_ctx, tok_rows, local_width = passthrough.shape
-    whole_in = lax.all_gather(passthrough, "head", axis=2, tiled=True)
+    back = jax.lax.axis_size("head")
+    y2 = jnp.stack(back * [passthrough])
+    kept_arr = jax.lax.all_to_all(y2, "head", 0, 0)
+    whole_in = jnp.concatenate(kept_arr, 2)
     widened = whole_in.astype(jnp.float32)
     full_width = widened.shape[2]
     inv_rms = lax.rsqrt(jnp.mean(widened * widened, axis=2, keepdims=True) + EPSILON)

time: 701 us -> 696 us (level)
  blocking collectives: 75.9 us -> 61.5 us
  starting transfers between devices: 0.16 us -> 9.6 us
    all_gather x1 -> x0, blocking collectives: 15.7 us -> none  [shards(): whole_in = lax.all_gather(passthrough, 'head', axis=2, tiled=True)]
    all_to_all x0 -> x1, starting transfers between devices: none -> 9.48 us  [shards(): kept_arr = jax.lax.all_to_all(y2, 'head', 0, 0)]
  transfers between devices with their start and end apart: 4 -> 5, of which waited for: 4 -> 5; matrix products, arithmetic and copies ran while one was open for 2% -> 2% of each run, Pallas kernels for 0% -> 0%
where the time goes in v1:
time: 696 us; the launch traced here: 695 us
  waiting for transfers between devices  469 us (67%)
  blocking collectives  61.5 us (9%)
  loops' own time  61.4 us (9%)
  other arithmetic  39 us (6%)
  local copies, waits for them, and re-layouts  26.2 us (4%)
  between operations  15.4 us (2%)
  matrix products  12 us (2%)
  starting transfers between devices  9.6 us (1%)
    reduce_scatter x1, waiting for transfers between devices, shards(): lax.psum_scatter(jnp.einsum('ctr,ctj->rj', normed, grads_flat, preferred_...  257 us
    all_gather x2, waiting for transfers between devices, carried_in(): lax.all_gather(a.astype(kind), axis)  194 us
    another operation x2, loops' own time, carried_in(): return lax.fori_loop(0, ahead, one, state)  61.4 us
    unnamed x1, blocking collectives  51.8 us
    select_n x31, other arithmetic, join_state(): jnp.where(vacant, early_state, late_state + jnp.where(same_id, early_stat...  32.2 us
    dynamic_slice x31, local copies, waits for them, and re-layouts, one(): lax.dynamic_index_in_dim(a, source, 0, False).astype(own.dtype)  18.2 us
    reduce_scatter x1, waiting for transfers between devices, shards(): lax.psum_scatter(partial_value.astype(jnp.bfloat16), 'head', scatter_dime...  15.5 us
  transfers between devices with their start and end apart: 5, of which 5 were waited for; matrix products, arithmetic and copies ran while one was open for 2% of the time, Pallas kernels for 0%

profile of v1, /device:TPU:2, one launch (start us, length us, event | category | flops | bytes accessed | tf_op | source)
XLA Modules:
  0.0 694.6 jit_solution(11806769577624319898)
XLA Ops:
  7.2 1.1 copy.70
  9.1 9.5 %all-to-all-start = ((bf16[4,1,256,256]{2,3,1,0:T(8,128)(2,1)}), bf16[4,1,256,256]{2,3,1,0:T(8,128)(2,1)S(1)}, u32[]{:S(2)}, u32[]{:S(2)}) async-start(bf16[4,1,256,256]{2,3,1,0:T(8,128)(2,1)} %stack.2), calls=%async_computation | async-start | bytes 1048576 | tf_op jit(solution)/shard_map/all_to_all | solution.py:93
  19.8 2.0 compare_reduce_fusion.1
  21.8 3.4 all-to-all-done
  30.1 1.3 dynamic-slice
  32.9 51.8 %all-reduce.2 = (bf16[32]{0:T(256)(128)(2,1)S(1)}, bf16[32]{0:T(256)(128)(2,1)}) all-reduce(bf16[32]{0:T(256)(128)(2,1)S(1)} %dynamic-update-slice, bf16[32]{0:T(256)(128)(2,1)S(1)} %dynamic-update-slice.1), channel_id=1, replica_groups=mesh['seq'=32,'head'=4,'dp'=4] {'seq'}, use_global_device_ids=true, to_apply=%add | all-reduce | flops 64 | bytes 256
  85.8 16.4 %all-gather.5.cloned.1.call-done = bf16[64,256,128]{2,1,0:T(8,128)(2,1)} async-done(((bf16[2,256,128]{2,1,0:T(8,128)(2,1)}), bf16[64,256,128]{2,1,0:T(8,128)(2,1)}) %all-gather.5.cloned.1.call-update) | async-done | bytes 4194320 | tf_op jit(solution)/shard_map/all_gather | solution.py:15
  105.6 177.3 %all-gather.7.cloned.1.call-done = bf16[64,256,128]{2,1,0:T(8,128)(2,1)} async-done(((bf16[2,256,128]{2,1,0:T(8,128)(2,1)}), bf16[64,256,128]{2,1,0:T(8,128)(2,1)}) %all-gather.7.cloned.1.call-update) | async-done | bytes 4194320 | tf_op jit(solution)/shard_map/all_gather | solution.py:15
  283.0 111.8 %while.27 = (s32[]{:T(128)}, f32[1,2,256,128]{3,2,1,0:T(8,128)S(1)}, f32[1]{0:T(128)}, s32[]{:T(128)}, bf16[32,1]{0,1:T(2,128)(2,1)S(1)}, /*index=5*/bf16[32,1,2...) while((s32[]{:T(128)}, ...), condition=%wide.region_9.10_spmd, body=%wide.region_8.9_spmd.sunk | while | flops 262153 | bytes 655570 | solution.py:30
  285.6 1.0 fusion.111
  289.2 1.0 fusion.111
  292.8 1.0 fusion.111
  300.0 1.0 fusion.111
  303.6 1.0 fusion.111
  307.2 1.0 fusion.111
  310.8 1.0 fusion.111
  395.9 2.8 fusion.11
  398.7 2.3 convolution_multiply_fusion
  401.9 15.5 %reduce-scatter.3.cloned.1.call-done = bf16[1,256,256]{2,1,0:T(8,128)(2,1)} async-done(((bf16[1,256,1024]{2,1,0:T(8,128)(2,1)}), bf16[1,256,256]{2,1,0:T(8,128)(2,1)}) %reduce-scatter.3.cloned.1.call-update) | async-done | bytes 131088 | tf_op jit(solution)/shard_map/reduce_scatter | solution.py:185
  417.4 1.1 fusion.44
  418.5 9.7 %psum.7 = f32[1,256]{1,0:T(1,128)S(1)} all-reduce(f32[1,256]{1,0:T(1,128)S(1)} %bitcast.277), channel_id=1, replica_groups=mesh['seq'=32,'head'=4,'dp'=4] {'head'}, use_global_device_ids=true, to_apply=%region_13.14 | all-reduce | flops 256 | bytes 2048 | tf_op jit(solution)/shard_map/psum | solution.py:189
  428.3 1.7 fusion.47
  430.0 256.7 %reduce-scatter.5.cloned.1.call-done = f32[8,768]{1,0:T(8,128)} async-done(((f32[1024,768]{1,0:T(8,128)}), f32[8,768]{1,0:T(8,128)}) %reduce-scatter.5.cloned.1.call-update) | async-done | bytes 24592 | tf_op jit(solution)/shard_map/reduce_scatter | solution.py:198
  686.7 1.3 fusion.82
  (138 shorter events, 56.6 us)
Async XLA Ops:
  7.2 19.4 %copy-start = (bf16[2,128,256]{2,1,0:T(8,128)(2,1)S(1)}, bf16[2,128,256]{2,1,0:T(8,128)(2,1)}, u32[]{:S(2)}) copy-start(bf16[2,128,256]{2,1,0:T(8,128)(2,1)} %param.20) | copy-start | bytes 393220
  7.2 18.4 %copy-start.2 = (bf16[1024,256]{1,0:T(8,128)(2,1)S(1)}, bf16[1024,256]{1,0:T(8,128)(2,1)}, u32[]{:S(2)}) copy-start(bf16[1024,256]{1,0:T(8,128)(2,1)} %param.18) | copy-start | bytes 1572868
  9.1 16.9 %copy-start.3 = (bf16[1024,256]{1,0:T(8,128)(2,1)S(1)}, bf16[1024,256]{1,0:T(8,128)(2,1)}, u32[]{:S(2)}) copy-start(bf16[1024,256]{1,0:T(8,128)(2,1)} %param.19) | copy-start | bytes 1572868
  9.1 16.1 %all-to-all-start = ((bf16[4,1,256,256]{2,3,1,0:T(8,128)(2,1)}), bf16[4,1,256,256]{2,3,1,0:T(8,128)(2,1)S(1)}, u32[]{:S(2)}, u32[]{:S(2)}) async-start(bf16[4,1,256,256]{2,3,1,0:T(8,128)(2,1)} %stack.2), calls=%async_computation | async-start | bytes 1048576 | tf_op jit(solution)/shard_map/all_to_all | solution.py:93
  18.6 83.6 %all-gather.5.cloned.1.call-start = ((), (), s32[]{:S(2)}) async-start(), calls=%async_computation.5 | async-start | bytes 4325376 | tf_op jit(solution)/shard_map/all_gather | solution.py:15
  25.5 59.2 %copy-start.11 = (s32[1,256]{1,0:T(1,128)S(1)}, s32[1,256]{1,0:T(1,128)}, u32[]{:S(2)}) copy-start(s32[1,256]{1,0:T(1,128)} %param.21) | copy-start | bytes 3076
  25.5 59.3 %copy-start.4 = (bf16[1024,256]{1,0:T(8,128)(2,1)S(1)}, bf16[1024,256]{1,0:T(8,128)(2,1)}, u32[]{:S(2)}) copy-start(bf16[1024,256]{1,0:T(8,128)(2,1)} %param.17) | copy-start | bytes 1572868
  26.5 75.7 %copy-start.5 = (bf16[1,256,2,128]{3,1,2,0:T(8,128)(2,1)}, bf16[1,256,2,128]{3,1,2,0:T(8,128)(2,1)S(1)}, u32[]{:S(2)}) copy-start(bf16[1,256,2,128]{3,1,2,0:T(8,128)(2,1)S(1)} %copy.79) | copy-start | bytes 393220
  27.7 255.2 %all-gather.7.cloned.1.call-start = ((), (), s32[]{:S(2)}) async-start(), calls=%async_computation.6 | async-start | bytes 4325376 | tf_op jit(solution)/shard_map/all_gather | solution.py:15
  84.8 0.7 copy-start.9
  102.2 1.8 copy-start.10
  102.2 1.8 copy-start.6
  103.9 179.0 %copy-start.12 = (bf16[32]{0:T(256)(128)(2,1)S(1)}, bf16[32]{0:T(256)(128)(2,1)}, u32[]{:S(2)}) copy-start(bf16[32]{0:T(256)(128)(2,1)} %get-tuple-element.187) | copy-start | bytes 196
  104.0 313.5 %reduce-scatter.3.cloned.1.call-start = ((), (), s32[]{:S(2)}) async-start(), calls=%async_computation.3 | async-start | bytes 655360 | tf_op jit(solution)/shard_map/reduce_scatter | solution.py:185
  398.7 288.0 %reduce-scatter.5.cloned.1.call-start = ((), (), s32[]{:S(2)}) async-start(), calls=%async_computation.4 | async-start | bytes 3170304 | tf_op jit(solution)/shard_map/reduce_scatter | solution.py:198
  398.7 2.5 copy-start.7
  401.0 16.4 %copy-start.1 = (bf16[1,256,256]{2,1,0:T(8,128)(2,1)S(1)}, bf16[1,256,256]{2,1,0:T(8,128)(2,1)}, u32[]{:S(2)}) copy-start(bf16[1,256,256]{2,1,0:T(8,128)(2,1)} %param.13) | copy-start | bytes 393220
  401.0 27.2 %copy-start.8 = (bf16[1,256,256]{2,1,0:T(8,128)(2,1)S(1)}, bf16[1,256,256]{2,1,0:T(8,128)(2,1)}, u32[]{:S(2)}) copy-start(bf16[1,256,256]{2,1,0:T(8,128)(2,1)} %param.16) | copy-start | bytes 393220
Sparse Core Ops, SparseCore 0:
  27.9 74.2 all-gather.4
  104.9 178.0 all-gather.6
  398.8 18.5 reduce-scatter.2
  421.9 264.7 reduce-scatter.4
